TPU v7x, 512 devices: a whole 4x4x16 slice. The times are simulated.
512 devices in a mesh: dom: 64 (over x, z), orb: 8 (over y, core).
Axes of the slice: x: 4, y: 4, z: 16, core: 2. Of those that a mesh axis runs over, the one named last changes fastest.
Arguments:
- orbitals: bfloat16 [3072, 64, 512], P('dom', 'orb'), may hold values from -6 to 6
- adjoint_source: bfloat16 [3072, 64, 512], P('dom', 'orb'), may hold values from -6 to 6
- eigenvalues: float32 [64], P('orb'), may hold values from -1 to -0.25
- cell_scale: float32 [3072], P('dom'), may hold values from 0.4 to 1.6
- base_potential: float32 [3072, 512], P('dom'), may hold values from 0.5 to 1.5
- stiffness: bfloat16 [512, 512], replicated, may hold values from -1.5 to 1.5, as said below
- face_perm: int32 [3072, 64], P('dom'), may hold values from 0 to 63, each once within a row
- restrict: bfloat16 [512, 64], replicated, may hold values from -0.25 to 0.25
- prolong: bfloat16 [64, 512], replicated, may hold values from -0.75 to 0.75
- owner: int32 [3072, 1], P('dom'), may hold values from 0 to 63; in each aligned block of 48 rows (0 to 47, 48 to 95, ...) at most 2 rows name the same one
- pot_slot: int32 [3072], P('dom'), may hold values from 0 to 63
- potential: float32 [4096, 64], P('dom'), may hold values from -6 to 6
Outputs:
- adjoint: bfloat16 [3072, 64, 512], P('dom', 'orb')
- updated: float32 [4096, 64], P('dom')
- applied: bfloat16 [3072, 64, 512], P('dom', 'orb')
Inputs may be any that keep to these rules, and one draw needn't show every extreme that they name: In the rows of one device no owner is named by more than 2 cells. `face_perm`: each row is a permutation. `stiffness`: symmetric.
All inputs are finite; a program needn't handle non-finite values.
Results may differ from a plain program's by a relative error of at most 0.0027.
Values sent between devices are 32-bit elements; how exact they have to be, the bound alone decides.
No kernel may reach another device: no remote copies, remote signals or barrier semaphores. Data moves between devices by JAX's collectives and lax.ppermute only.
A program may use at most 64 MiB of HBM per device.

v0:
```python
import jax
import jax.numpy as jnp
from jax import lax
from jax.sharding import PartitionSpec as P

ITERS = 4
relax = 0.25
step_rate = 0.1


def padded_2(block, sides, width):
    for axis, dim in sides:
        count = lax.axis_size(axis)
        forward = [(i, i + 1) for i in range(count - 1)]
        backward = [(target, source) for source, target in forward]
        low = lax.ppermute(
            lax.slice_in_dim(block, block.shape[dim] - width, None, axis=dim), axis, forward
        )
        high = lax.ppermute(lax.slice_in_dim(block, 0, width, axis=dim), axis, backward)
        block = jnp.concatenate([low, block, high], axis=dim)
    return block


def local(
    orbitals,
    adjoint_source,
    eigenvalues,
    cell_scale,
    base_potential,
    stiffness,
    face_perm,
    restrict,
    prolong,
    owner,
    pot_slot,
    potential,
):
    nodes = stiffness.shape[0]
    faces = face_perm.shape[1]
    pot_rows = potential.shape[0]
    n_domains = lax.axis_size("dom")
    cell_count = owner.shape[0]
    capacity = 2 * ((cell_count + n_domains - 1) // n_domains)
    onehot = (face_perm[:, :, None] == jnp.arange(faces, dtype=jnp.int32)[None, None, :]).astype(
        jnp.float32
    )

    def assemble_local(partial_sum):
        left_face = partial_sum[:, :, :faces]
        right_face = partial_sum[:, :, nodes - faces :]
        sent_right = jnp.einsum("ckj,cok->coj", onehot, right_face, precision=lax.Precision.HIGHEST)
        boundary = jnp.stack([left_face[0], sent_right[-1]], 0)
        padded = padded_2(boundary, (("dom", 0),), 1)
        left_next = jnp.concatenate([left_face[1:], padded[3][None]], 0)
        add_right = jnp.einsum("ckj,coj->cok", onehot, left_next, precision=lax.Precision.HIGHEST)
        add_left = jnp.concatenate([padded[0][None], sent_right[:-1]], 0)
        return jnp.concatenate(
            [
                left_face + add_left,
                partial_sum[:, :, faces : nodes - faces],
                right_face + add_right,
            ],
            2,
        )

    def operator(values_bf, values_full, shift):
        kinetic = jnp.dot(
            values_bf.reshape(-1, nodes), stiffness, preferred_element_type=jnp.float32
        ).reshape(values_full.shape)
        return assemble_local(cell_scale[:, None, None] * kinetic + shift * values_full)

    source = adjoint_source.astype(jnp.float32)
    shift = base_potential[:, None, :] - eigenvalues[None, :, None]
    iterate = relax * source
    for step_index in range(ITERS):
        image = operator(iterate.astype(jnp.bfloat16), iterate, shift)
        iterate = iterate + relax * (source - image)
    adjoint = iterate.astype(jnp.bfloat16)
    partial_density = jnp.sum(orbitals.astype(jnp.float32) * iterate, axis=1)
    restrict_full = restrict.astype(jnp.float32)
    density_term = lax.psum(partial_density, "orb")
    projected = jnp.dot(density_term, restrict_full, precision=lax.Precision.HIGHEST)
    coarse_cols = projected.shape[1]
    dest_owner = owner[:, 0]
    owner_hot = (dest_owner[:, None] == jnp.arange(n_domains, dtype=jnp.int32)[None, :]).astype(
        jnp.int32
    )
    earlier = jnp.cumsum(owner_hot, axis=0) - owner_hot
    rank_within = jnp.sum(earlier * owner_hot, axis=1)
    slot_index = dest_owner * capacity + rank_within
    send_hot_int = (
        slot_index[None, :] == jnp.arange(n_domains * capacity, dtype=jnp.int32)[:, None]
    ).astype(jnp.int32)
    send_hot = send_hot_int.astype(jnp.float32)
    send_values = jnp.dot(send_hot, projected, precision=lax.Precision.HIGHEST).reshape(
        n_domains, capacity, coarse_cols
    )
    send_ids = (jnp.sum(send_hot_int * (pot_slot + 1)[None, :], axis=1) - 1).reshape(
        n_domains, capacity
    )
    recv_values, recv_ids = (
        lax.all_to_all(send_values, "dom", split_axis=0, concat_axis=0, tiled=True),
        lax.all_to_all(send_ids, "dom", split_axis=0, concat_axis=0, tiled=True),
    )
    recv_hot = (
        recv_ids.reshape(-1)[None, :] == jnp.arange(pot_rows, dtype=jnp.int32)[:, None]
    ).astype(jnp.float32)
    summed = jnp.dot(
        recv_hot, recv_values.reshape(-1, coarse_cols), precision=lax.Precision.HIGHEST
    )
    updated = potential - step_rate * summed
    every_pot = lax.all_gather(updated, "dom", axis=0, tiled=True)
    cell_pot = every_pot[dest_owner * pot_rows + pot_slot]
    node_potential = jnp.dot(cell_pot, prolong.astype(jnp.float32), precision=lax.Precision.HIGHEST)
    shift_new = (base_potential + node_potential)[:, None, :]
    applied = operator(orbitals, orbitals.astype(jnp.float32), shift_new).astype(jnp.bfloat16)
    return (adjoint, updated, applied)


def solution(mesh):
    in_specs = (
        P("dom", "orb", None),
        P("dom", "orb", None),
        P("orb"),
        P("dom"),
        P("dom", None),
        P(),
        P("dom", None),
        P(),
        P(),
        P("dom", None),
        P("dom"),
        P("dom", None),
    )
    out_specs = (P("dom", "orb", None), P("dom", None), P("dom", "orb", None))
    return jax.shard_map(local, mesh=mesh, in_specs=in_specs, out_specs=out_specs, check_vma=False)
```

profile of v0, /device:TPU:2, one launch (start us, length us, event | category | flops | bytes accessed | tf_op | source)
XLA Modules:
  0.0 320.8 jit_solution(6365384118985894531)
XLA Ops:
  7.3 1.0 copy-done
  8.2 1.6 fusion.10
  9.8 11.4 %collective-permute-start.1 = (f32[1,8,64]{2,1,0:T(8,128)S(1)}, f32[1,8,64]{2,1,0:T(8,128)S(1)}, u32[]{:S(2)}, u32[]{:S(2)}) collective-permute-start(f32[1,8,64]{2,1,0:T(8,128)S(1)} %slice.159), channel_id=1, source_target_pairs={{8,0},{16,8},{24,16},{32,24},{40,32},{48,40},{56,48},{64,56},{72,6... | collective-permute-start | bytes 6152 | tf_op jit(solution)/shard_map/ppermute | solution.py:19
  21.2 1.4 fusion.9
  22.7 1.9 collective-permute-start
  25.4 1.4 fusion.15
  26.8 3.5 %collective-permute-done = f32[1,8,64]{2,1,0:T(8,128)S(1)} collective-permute-done((f32[1,8,64]{2,1,0:T(8,128)S(1)}, f32[1,8,64]{2,1,0:T(8,128)S(1)}, u32[]{:S(2)}, u32[]{:S(2)}) %collective-permute-start) | collective-permute-done | bytes 2080 | tf_op jit(solution)/shard_map/ppermute | solution.py:16
  30.3 0.8 fusion.11
  31.2 2.6 collective-permute-start.3
  33.8 1.4 fusion.7
  35.5 3.3 %collective-permute-start.2 = (f32[1,8,64]{2,1,0:T(8,128)S(1)}, f32[1,8,64]{2,1,0:T(8,128)S(1)}, u32[]{:S(2)}, u32[]{:S(2)}) collective-permute-start(f32[1,8,64]{2,1,0:T(8,128)S(1)} %slice.162), channel_id=1, source_target_pairs={{0,8},{8,16},{16,24},{24,32},{32,40},{40,48},{48,56},{56,64},{64,7... | collective-permute-start | bytes 6152 | tf_op jit(solution)/shard_map/ppermute | solution.py:16
  38.8 1.4 fusion.16
  40.2 2.9 collective-permute-done.2
  43.2 0.6 fusion.27
  43.8 0.4 fusion.12
  44.2 1.9 collective-permute-start.5
  46.1 1.4 fusion.5
  47.8 3.9 %collective-permute-start.4 = (f32[1,8,64]{2,1,0:T(8,128)S(1)}, f32[1,8,64]{2,1,0:T(8,128)S(1)}, u32[]{:S(2)}, u32[]{:S(2)}) collective-permute-start(f32[1,8,64]{2,1,0:T(8,128)S(1)} %slice.169), channel_id=1, source_target_pairs={{0,8},{8,16},{16,24},{24,32},{32,40},{40,48},{48,56},{56,64},{64,7... | collective-permute-start | bytes 6152 | tf_op jit(solution)/shard_map/ppermute | solution.py:16
  51.8 1.4 fusion.17
  53.2 2.3 collective-permute-done.4
  55.5 0.8 fusion.13
  56.3 1.9 collective-permute-start.7
  58.3 1.4 fusion.3
  60.0 3.9 %collective-permute-start.6 = (f32[1,8,64]{2,1,0:T(8,128)S(1)}, f32[1,8,64]{2,1,0:T(8,128)S(1)}, u32[]{:S(2)}, u32[]{:S(2)}) collective-permute-start(f32[1,8,64]{2,1,0:T(8,128)S(1)} %slice.176), channel_id=1, source_target_pairs={{0,8},{8,16},{16,24},{24,32},{32,40},{40,48},{48,56},{56,64},{64,7... | collective-permute-start | bytes 6152 | tf_op jit(solution)/shard_map/ppermute | solution.py:16
  63.9 1.4 fusion.18
  65.3 2.3 collective-permute-done.6
  67.7 2.1 fusion.24
  69.8 0.8 sub.46
  70.5 5.7 %all-to-all-start = ((s32[64,1,2]{2,1,0:T(1,128)}), s32[64,1,2]{2,1,0:T(1,128)S(1)}, u32[]{:S(2)}, u32[]{:S(2)}) async-start(s32[64,1,2]{2,1,0:T(1,128)} %bitcast.2), calls=%async_computation | async-start | bytes 65536 | tf_op jit(solution)/shard_map/all_to_all | solution.py:103
  76.3 58.1 %all-reduce.2.cloned.1.call-done = f32[48,512]{1,0:T(8,128)} async-done(((f32[48,512]{1,0:T(8,128)}), f32[48,512]{1,0:T(8,128)}) %all-reduce.2.cloned.1.call-update) | async-done | bytes 98320 | tf_op jit(solution)/shard_map/psum | solution.py:81
  134.3 1.1 fusion.90
  135.8 0.7 reshape.85
  136.5 15.9 %all-to-all-start.1 = ((f32[64,1,128]{2,1,0:T(1,128)}), f32[64,1,128]{2,1,0:T(1,128)S(1)}, u32[]{:S(2)}, u32[]{:S(2)}) async-start(f32[64,1,128]{2,1,0:T(1,128)} %reshape.85), calls=%async_computation.1 | async-start | bytes 65536 | tf_op jit(solution)/shard_map/all_to_all | solution.py:102
  152.5 0.5 broadcast.70
  153.0 0.7 reduce.3
  153.8 12.0 %all-to-all-done.1 = f32[64,1,128]{2,1,0:T(1,128)S(1)} async-done(((f32[64,1,128]{2,1,0:T(1,128)}), f32[64,1,128]{2,1,0:T(1,128)S(1)}, u32[]{:S(2)}, u32[]{:S(2)}) %all-to-all-start.1) | async-done | bytes 32800 | tf_op jit(solution)/shard_map/all_to_all | solution.py:102
  165.9 0.5 broadcast.72
  166.4 0.7 reduce.4
  167.2 0.8 fusion.21
  168.0 128.1 %all-gather.2.cloned.1.call-done = f32[4096,64]{1,0:T(8,128)} async-done(((f32[64,64]{1,0:T(8,128)}), f32[4096,64]{1,0:T(8,128)}) %all-gather.2.cloned.1.call-update) | async-done | bytes 1048592 | tf_op jit(solution)/shard_map/all_gather | solution.py:112
  296.1 2.2 gather_fusion
  298.5 0.4 fusion.14
  298.9 4.8 %collective-permute-start.9 = (f32[1,8,64]{2,1,0:T(8,128)S(1)}, f32[1,8,64]{2,1,0:T(8,128)S(1)}, u32[]{:S(2)}, u32[]{:S(2)}) collective-permute-start(f32[1,8,64]{2,1,0:T(8,128)S(1)} %slice.187), channel_id=1, source_target_pairs={{8,0},{16,8},{24,16},{32,24},{40,32},{48,40},{56,48},{64,56},{72,6... | collective-permute-start | bytes 6152 | tf_op jit(solution)/shard_map/ppermute | solution.py:19
  303.7 1.4 fusion.1
  305.4 1.9 collective-permute-start.8
  307.3 1.6 fusion.20
  308.9 4.1 %collective-permute-done.8 = f32[1,8,64]{2,1,0:T(8,128)S(1)} collective-permute-done((f32[1,8,64]{2,1,0:T(8,128)S(1)}, f32[1,8,64]{2,1,0:T(8,128)S(1)}, u32[]{:S(2)}, u32[]{:S(2)}) %collective-permute-start.8) | collective-permute-done | bytes 2080 | tf_op jit(solution)/shard_map/ppermute | solution.py:16
  313.0 1.0 pad_maximum_fusion
  (74 shorter events, 2.8 us)
Async XLA Ops:
  7.2 1.0 copy-start
  7.2 14.0 %copy-start.11 = (s32[48,64]{1,0:T(8,128)S(1)}, s32[48,64]{1,0:T(8,128)}, u32[]{:S(2)}) copy-start(s32[48,64]{1,0:T(8,128)} %param.18) | copy-start | bytes 36868
  7.2 17.4 %copy-start.7 = (s32[48,1]{0,1:T(1,128)S(1)}, s32[48,1]{0,1:T(1,128)}, u32[]{:S(2)}) copy-start(s32[48,1]{0,1:T(1,128)} %param.21) | copy-start | bytes 580
  7.2 17.7 %copy-start.9 = (s32[48]{0:T(128)S(1)}, s32[48]{0:T(128)}, u32[]{:S(2)}) copy-start(s32[48]{0:T(128)} %param.22) | copy-start | bytes 580
  7.2 127.1 %all-reduce.2.cloned.1.call-start = ((), (), s32[]{:S(2)}) async-start(), calls=%async_computation.2 | async-start | bytes 196608 | tf_op jit(solution)/shard_map/psum | solution.py:81
  9.8 15.5 %collective-permute-start.1 = (f32[1,8,64]{2,1,0:T(8,128)S(1)}, f32[1,8,64]{2,1,0:T(8,128)S(1)}, u32[]{:S(2)}, u32[]{:S(2)}) collective-permute-start(f32[1,8,64]{2,1,0:T(8,128)S(1)} %slice.159), channel_id=1, source_target_pairs={{8,0},{16,8},{24,16},{32,24},{40,32},{48,40},{56,48},{64,56},{72,6... | collective-permute-start | bytes 6152 | tf_op jit(solution)/shard_map/ppermute | solution.py:19
  22.7 7.6 %collective-permute-start = (f32[1,8,64]{2,1,0:T(8,128)S(1)}, f32[1,8,64]{2,1,0:T(8,128)S(1)}, u32[]{:S(2)}, u32[]{:S(2)}) collective-permute-start(f32[1,8,64]{2,1,0:T(8,128)S(1)} %slice.155), channel_id=1, source_target_pairs={{0,8},{8,16},{16,24},{24,32},{32,40},{40,48},{48,56},{56,64},{64,7... | collective-permute-start | bytes 6152 | tf_op jit(solution)/shard_map/ppermute | solution.py:16
  25.0 5.3 %copy-start.1 = (bf16[48,8,512]{2,1,0:T(8,128)(2,1)S(1)}, bf16[48,8,512]{2,1,0:T(8,128)(2,1)}, u32[]{:S(2)}) copy-start(bf16[48,8,512]{2,1,0:T(8,128)(2,1)} %param.13) | copy-start | bytes 1179652
  25.1 5.3 %copy-start.3 = (f32[48,512]{1,0:T(8,128)S(1)}, f32[48,512]{1,0:T(8,128)}, u32[]{:S(2)}) copy-start(f32[48,512]{1,0:T(8,128)} %param.16) | copy-start | bytes 294916
  25.1 5.3 %copy-start.8 = (f32[48]{0:T(128)S(1)}, f32[48]{0:T(128)}, u32[]{:S(2)}) copy-start(f32[48]{0:T(128)} %param.15) | copy-start | bytes 580
  25.1 5.3 %copy-start.10 = (f32[8]{0:T(128)S(1)}, f32[8]{0:T(128)}, u32[]{:S(2)}) copy-start(f32[8]{0:T(128)} %param.14) | copy-start | bytes 100
  31.2 7.6 %collective-permute-start.3 = (f32[1,8,64]{2,1,0:T(8,128)S(1)}, f32[1,8,64]{2,1,0:T(8,128)S(1)}, u32[]{:S(2)}, u32[]{:S(2)}) collective-permute-start(f32[1,8,64]{2,1,0:T(8,128)S(1)} %slice.166), channel_id=1, source_target_pairs={{8,0},{16,8},{24,16},{32,24},{40,32},{48,40},{56,48},{64,56},{72,6... | collective-permute-start | bytes 6152 | tf_op jit(solution)/shard_map/ppermute | solution.py:19
  35.5 7.6 %collective-permute-start.2 = (f32[1,8,64]{2,1,0:T(8,128)S(1)}, f32[1,8,64]{2,1,0:T(8,128)S(1)}, u32[]{:S(2)}, u32[]{:S(2)}) collective-permute-start(f32[1,8,64]{2,1,0:T(8,128)S(1)} %slice.162), channel_id=1, source_target_pairs={{0,8},{8,16},{16,24},{24,32},{32,40},{40,48},{48,56},{56,64},{64,7... | collective-permute-start | bytes 6152 | tf_op jit(solution)/shard_map/ppermute | solution.py:16
  44.2 7.6 %collective-permute-start.5 = (f32[1,8,64]{2,1,0:T(8,128)S(1)}, f32[1,8,64]{2,1,0:T(8,128)S(1)}, u32[]{:S(2)}, u32[]{:S(2)}) collective-permute-start(f32[1,8,64]{2,1,0:T(8,128)S(1)} %slice.173), channel_id=1, source_target_pairs={{8,0},{16,8},{24,16},{32,24},{40,32},{48,40},{56,48},{64,56},{72,6... | collective-permute-start | bytes 6152 | tf_op jit(solution)/shard_map/ppermute | solution.py:19
  47.8 7.6 %collective-permute-start.4 = (f32[1,8,64]{2,1,0:T(8,128)S(1)}, f32[1,8,64]{2,1,0:T(8,128)S(1)}, u32[]{:S(2)}, u32[]{:S(2)}) collective-permute-start(f32[1,8,64]{2,1,0:T(8,128)S(1)} %slice.169), channel_id=1, source_target_pairs={{0,8},{8,16},{16,24},{24,32},{32,40},{40,48},{48,56},{56,64},{64,7... | collective-permute-start | bytes 6152 | tf_op jit(solution)/shard_map/ppermute | solution.py:16
  56.3 7.6 %collective-permute-start.7 = (f32[1,8,64]{2,1,0:T(8,128)S(1)}, f32[1,8,64]{2,1,0:T(8,128)S(1)}, u32[]{:S(2)}, u32[]{:S(2)}) collective-permute-start(f32[1,8,64]{2,1,0:T(8,128)S(1)} %slice.180), channel_id=1, source_target_pairs={{8,0},{16,8},{24,16},{32,24},{40,32},{48,40},{56,48},{64,56},{72,6... | collective-permute-start | bytes 6152 | tf_op jit(solution)/shard_map/ppermute | solution.py:19
  59.7 8.0 %copy-start.2 = (bf16[48,8,512]{2,1,0:T(8,128)(2,1)S(1)}, bf16[48,8,512]{2,1,0:T(8,128)(2,1)}, u32[]{:S(2)}) copy-start(bf16[48,8,512]{2,1,0:T(8,128)(2,1)} %param.12) | copy-start | bytes 1179652
  60.0 7.6 %collective-permute-start.6 = (f32[1,8,64]{2,1,0:T(8,128)S(1)}, f32[1,8,64]{2,1,0:T(8,128)S(1)}, u32[]{:S(2)}, u32[]{:S(2)}) collective-permute-start(f32[1,8,64]{2,1,0:T(8,128)S(1)} %slice.176), channel_id=1, source_target_pairs={{0,8},{8,16},{16,24},{24,32},{32,40},{40,48},{48,56},{56,64},{64,7... | collective-permute-start | bytes 6152 | tf_op jit(solution)/shard_map/ppermute | solution.py:16
  67.6 66.7 %copy-start.4 = (bf16[512,64]{0,1:T(8,128)(2,1)S(1)}, bf16[512,64]{0,1:T(8,128)(2,1)}, u32[]{:S(2)}) copy-start(bf16[512,64]{0,1:T(8,128)(2,1)} %param.19) | copy-start | bytes 196612
  67.7 99.5 %copy-start.6 = (f32[64,64]{1,0:T(8,128)S(1)}, f32[64,64]{1,0:T(8,128)}, u32[]{:S(2)}) copy-start(f32[64,64]{1,0:T(8,128)} %param.23) | copy-start | bytes 49156
  67.7 230.6 %copy-start.5 = (bf16[64,512]{1,0:T(8,128)(2,1)S(1)}, bf16[64,512]{1,0:T(8,128)(2,1)}, u32[]{:S(2)}) copy-start(bf16[64,512]{1,0:T(8,128)(2,1)} %param.20) | copy-start | bytes 196612
  70.5 65.9 %all-to-all-start = ((s32[64,1,2]{2,1,0:T(1,128)}), s32[64,1,2]{2,1,0:T(1,128)S(1)}, u32[]{:S(2)}, u32[]{:S(2)}) async-start(s32[64,1,2]{2,1,0:T(1,128)} %bitcast.2), calls=%async_computation | async-start | bytes 65536 | tf_op jit(solution)/shard_map/all_to_all | solution.py:103
  136.5 29.4 %all-to-all-start.1 = ((f32[64,1,128]{2,1,0:T(1,128)}), f32[64,1,128]{2,1,0:T(1,128)S(1)}, u32[]{:S(2)}, u32[]{:S(2)}) async-start(f32[64,1,128]{2,1,0:T(1,128)} %reshape.85), calls=%async_computation.1 | async-start | bytes 65536 | tf_op jit(solution)/shard_map/all_to_all | solution.py:102
  152.4 143.7 %all-gather.2.cloned.1.call-start = ((), (), s32[]{:S(2)}) async-start(), calls=%async_computation.3 | async-start | bytes 2129920 | tf_op jit(solution)/shard_map/all_gather | solution.py:112
  298.9 8.4 %collective-permute-start.9 = (f32[1,8,64]{2,1,0:T(8,128)S(1)}, f32[1,8,64]{2,1,0:T(8,128)S(1)}, u32[]{:S(2)}, u32[]{:S(2)}) collective-permute-start(f32[1,8,64]{2,1,0:T(8,128)S(1)} %slice.187), channel_id=1, source_target_pairs={{8,0},{16,8},{24,16},{32,24},{40,32},{48,40},{56,48},{64,56},{72,6... | collective-permute-start | bytes 6152 | tf_op jit(solution)/shard_map/ppermute | solution.py:19
  305.4 7.6 %collective-permute-start.8 = (f32[1,8,64]{2,1,0:T(8,128)S(1)}, f32[1,8,64]{2,1,0:T(8,128)S(1)}, u32[]{:S(2)}, u32[]{:S(2)}) collective-permute-start(f32[1,8,64]{2,1,0:T(8,128)S(1)} %slice.183), channel_id=1, source_target_pairs={{0,8},{8,16},{16,24},{24,32},{32,40},{40,48},{48,56},{56,64},{64,7... | collective-permute-start | bytes 6152 | tf_op jit(solution)/shard_map/ppermute | solution.py:16
Sparse Core Ops, SparseCore 0:
  69.9 64.3 all-reduce.1
  168.1 127.9 all-gather.1
where the time goes:
time: 321 us
  waiting for transfers between devices  213 us (66%)
  starting transfers between devices  59.2 us (18%)
  matrix products  20.7 us (6%)
  between operations  14.7 us (5%)
  local copies, waits for them, and re-layouts  7.21 us (2%)
  other arithmetic  5.72 us (2%)
    all_gather x1, waiting for transfers between devices, local(): every_pot = lax.all_gather(updated, 'dom', axis=0, tiled=True)  128 us
    psum x1, waiting for transfers between devices, local(): density_term = lax.psum(partial_density, 'orb')  58.1 us
    ppermute x5, starting transfers between devices, padded_2(): lax.ppermute(lax.slice_in_dim(block, 0, width, axis=dim), axis, backward)  22.6 us
    all_to_all x1, starting transfers between devices, local(): lax.all_to_all(send_values, 'dom', split_axis=0, concat_axis=0, tiled=True)  15.9 us
    ppermute x5, waiting for transfers between devices, padded_2(): lax.ppermute(lax.slice_in_dim(block, block.shape[dim] - width, None, axis...  15 us
    ppermute x5, starting transfers between devices, padded_2(): lax.ppermute(lax.slice_in_dim(block, block.shape[dim] - width, None, axis...  15 us
    all_to_all x1, waiting for transfers between devices, local(): lax.all_to_all(send_values, 'dom', split_axis=0, concat_axis=0, tiled=True)  12 us
    dot_general x5, matrix products, assemble_local(): jnp.einsum('ckj,coj->cok', onehot, left_next, precision=lax.Precision.HIG...  7.2 us
  transfers between devices with their start and end apart: 14, of which 8 were waited for; matrix products, arithmetic and copies ran while one was open for 6% of the time, Pallas kernels for 0%

commit v1 on v0

--- a/solution.py
+++ b/solution.py
@@ -78,7 +78,11 @@
     adjoint = iterate.astype(jnp.bfloat16)
     partial_density = jnp.sum(orbitals.astype(jnp.float32) * iterate, axis=1)
     restrict_full = restrict.astype(jnp.float32)
-    density_term = lax.psum(partial_density, "orb")
+    density_term = partial_density
+    for hop in (1, 2, 4):
+        density_term = density_term + lax.ppermute(
+            density_term, "orb", [(dev, dev ^ hop) for dev in range(8)]
+        )
     projected = jnp.dot(density_term, restrict_full, precision=lax.Precision.HIGHEST)
     coarse_cols = projected.shape[1]
     dest_owner = owner[:, 0]

time: 321 us -> 279 us (0.87)
  waiting for transfers between devices: 213 us -> 172 us
    psum x1 -> x0, waiting for transfers between devices: 58.1 us -> none  [local(): density_term = lax.psum(partial_density, 'orb')]
    all_to_all x1, waiting for transfers between devices: 0.01 us -> 12.2 us  [local(): lax.all_to_all(send_ids, 'dom', split_axis=0, concat_axis=0, tiled=True)]
    ppermute x0 -> x3, starting transfers between devices: none -> 10.6 us  [local(): lax.ppermute(density_term, 'orb', [(dev, dev ^ hop) for dev in range(8)])]
    all_to_all x1, starting transfers between devices: 15.9 us -> 5.66 us  [local(): lax.all_to_all(send_values, 'dom', split_axis=0, concat_axis=0, tiled=True)]
    ppermute x0 -> x3, waiting for transfers between devices: none -> 4.4 us  [local(): lax.ppermute(density_term, 'orb', [(dev, dev ^ hop) for dev in range(8)])]
  transfers between devices with their start and end apart: 14 -> 16, of which waited for: 8 -> 10; matrix products, arithmetic and copies ran while one was open for 6% -> 7% of each run, Pallas kernels for 0% -> 0%
where the time goes in v1:
time: 279 us
  waiting for transfers between devices  172 us (62%)
  starting transfers between devices  59.6 us (21%)
  matrix products  19.8 us (7%)
  between operations  14.7 us (5%)
  local copies, waits for them, and re-layouts  7.27 us (3%)
  other arithmetic  5.11 us (2%)
    all_gather x1, waiting for transfers between devices, local(): every_pot = lax.all_gather(updated, 'dom', axis=0, tiled=True)  129 us
    ppermute x5, starting transfers between devices, padded_2(): lax.ppermute(lax.slice_in_dim(block, 0, width, axis=dim), axis, backward)  22.5 us
    ppermute x5, starting transfers between devices, padded_2(): lax.ppermute(lax.slice_in_dim(block, block.shape[dim] - width, None, axis...  15.1 us
    ppermute x5, waiting for transfers between devices, padded_2(): lax.ppermute(lax.slice_in_dim(block, block.shape[dim] - width, None, axis...  15 us
    all_to_all x1, waiting for transfers between devices, local(): lax.all_to_all(send_ids, 'dom', split_axis=0, concat_axis=0, tiled=True)  12.2 us
    all_to_all x1, waiting for transfers between devices, local(): lax.all_to_all(send_values, 'dom', split_axis=0, concat_axis=0, tiled=True)  12 us
    ppermute x3, starting transfers between devices, local(): lax.ppermute(density_term, 'orb', [(dev, dev ^ hop) for dev in range(8)])  10.6 us
    dot_general x5, matrix products, assemble_local(): jnp.einsum('ckj,coj->cok', onehot, left_next, precision=lax.Precision.HIG...  7.2 us
  transfers between devices with their start and end apart: 16, of which 10 were waited for; matrix products, arithmetic and copies ran while one was open for 7% of the time, Pallas kernels for 0%

profile of v1, /device:TPU:2, one launch (start us, length us, event | category | flops | bytes accessed | tf_op | source)
XLA Modules:
  0.0 278.8 jit_solution(17125449044378127406)
XLA Ops:
  7.2 1.0 copy-done
  8.2 1.6 fusion.10
  9.8 11.4 %collective-permute-start.1 = (f32[1,8,64]{2,1,0:T(8,128)S(1)}, f32[1,8,64]{2,1,0:T(8,128)S(1)}, u32[]{:S(2)}, u32[]{:S(2)}) collective-permute-start(f32[1,8,64]{2,1,0:T(8,128)S(1)} %slice.159), channel_id=1, source_target_pairs={{8,0},{16,8},{24,16},{32,24},{40,32},{48,40},{56,48},{64,56},{72,6... | collective-permute-start | bytes 6152 | tf_op jit(solution)/shard_map/ppermute | solution.py:19
  21.2 1.4 fusion.9
  22.7 1.9 collective-permute-start
  25.3 1.4 fusion.15
  26.7 3.6 %collective-permute-done = f32[1,8,64]{2,1,0:T(8,128)S(1)} collective-permute-done((f32[1,8,64]{2,1,0:T(8,128)S(1)}, f32[1,8,64]{2,1,0:T(8,128)S(1)}, u32[]{:S(2)}, u32[]{:S(2)}) %collective-permute-start) | collective-permute-done | bytes 2080 | tf_op jit(solution)/shard_map/ppermute | solution.py:16
  30.3 0.8 fusion.11
  31.2 2.4 collective-permute-start.3
  33.7 1.4 fusion.7
  35.4 3.4 %collective-permute-start.2 = (f32[1,8,64]{2,1,0:T(8,128)S(1)}, f32[1,8,64]{2,1,0:T(8,128)S(1)}, u32[]{:S(2)}, u32[]{:S(2)}) collective-permute-start(f32[1,8,64]{2,1,0:T(8,128)S(1)} %slice.162), channel_id=1, source_target_pairs={{0,8},{8,16},{16,24},{24,32},{32,40},{40,48},{48,56},{56,64},{64,7... | collective-permute-start | bytes 6152 | tf_op jit(solution)/shard_map/ppermute | solution.py:16
  38.8 1.4 fusion.16
  40.2 2.8 %collective-permute-done.2 = f32[1,8,64]{2,1,0:T(8,128)S(1)} collective-permute-done((f32[1,8,64]{2,1,0:T(8,128)S(1)}, f32[1,8,64]{2,1,0:T(8,128)S(1)}, u32[]{:S(2)}, u32[]{:S(2)}) %collective-permute-start.2) | collective-permute-done | bytes 2080 | tf_op jit(solution)/shard_map/ppermute | solution.py:16
  43.0 0.6 fusion.27
  44.1 1.9 collective-permute-start.5
  46.0 1.4 fusion.5
  47.7 3.9 %collective-permute-start.4 = (f32[1,8,64]{2,1,0:T(8,128)S(1)}, f32[1,8,64]{2,1,0:T(8,128)S(1)}, u32[]{:S(2)}, u32[]{:S(2)}) collective-permute-start(f32[1,8,64]{2,1,0:T(8,128)S(1)} %slice.169), channel_id=1, source_target_pairs={{0,8},{8,16},{16,24},{24,32},{32,40},{40,48},{48,56},{56,64},{64,7... | collective-permute-start | bytes 6152 | tf_op jit(solution)/shard_map/ppermute | solution.py:16
  51.7 1.4 fusion.17
  53.1 2.3 collective-permute-done.4
  55.4 0.8 fusion.13
  56.2 1.9 collective-permute-start.7
  58.1 1.4 fusion.3
  59.9 3.9 %collective-permute-start.6 = (f32[1,8,64]{2,1,0:T(8,128)S(1)}, f32[1,8,64]{2,1,0:T(8,128)S(1)}, u32[]{:S(2)}, u32[]{:S(2)}) collective-permute-start(f32[1,8,64]{2,1,0:T(8,128)S(1)} %slice.176), channel_id=1, source_target_pairs={{0,8},{8,16},{16,24},{24,32},{32,40},{40,48},{48,56},{56,64},{64,7... | collective-permute-start | bytes 6152 | tf_op jit(solution)/shard_map/ppermute | solution.py:16
  63.8 1.4 fusion.18
  65.2 2.3 collective-permute-done.6
  67.6 1.4 fusion.24
  69.0 2.0 collective-permute-start.8
  71.1 1.2 collective-permute-done.8
  72.3 3.5 %collective-permute-start.9 = (f32[48,512]{1,0:T(8,128)S(1)}, f32[48,512]{1,0:T(8,128)S(1)}, u32[]{:S(2)}, u32[]{:S(2)}) collective-permute-start(f32[48,512]{1,0:T(8,128)S(1)} %add.120), channel_id=1, source_target_pairs={{0,2},{1,3},{2,0},{3,1},{4,6},{5,7},{6,4},{7,5},{8,10},{9,11},{10,... | collective-permute-start | bytes 294920 | tf_op jit(solution)/shard_map/ppermute | solution.py:83
  75.9 3.2 %collective-permute-done.9 = f32[48,512]{1,0:T(8,128)S(1)} collective-permute-done((f32[48,512]{1,0:T(8,128)S(1)}, f32[48,512]{1,0:T(8,128)S(1)}, u32[]{:S(2)}, u32[]{:S(2)}) %collective-permute-start.9) | collective-permute-done | bytes 98336 | tf_op jit(solution)/shard_map/ppermute | solution.py:83
  79.1 5.1 %collective-permute-start.10 = (f32[48,512]{1,0:T(8,128)S(1)}, f32[48,512]{1,0:T(8,128)S(1)}, u32[]{:S(2)}, u32[]{:S(2)}) collective-permute-start(f32[48,512]{1,0:T(8,128)S(1)} %add.121), channel_id=1, source_target_pairs={{0,4},{1,5},{2,6},{3,7},{4,0},{5,1},{6,2},{7,3},{8,12},{9,13},{10,... | collective-permute-start | bytes 294920 | tf_op jit(solution)/shard_map/ppermute | solution.py:83
  84.2 0.8 sub.46
  85.0 5.7 %all-to-all-start = ((s32[64,1,2]{2,1,0:T(1,128)}), s32[64,1,2]{2,1,0:T(1,128)S(1)}, u32[]{:S(2)}, u32[]{:S(2)}) async-start(s32[64,1,2]{2,1,0:T(1,128)} %bitcast.2), calls=%async_computation | async-start | bytes 65536 | tf_op jit(solution)/shard_map/all_to_all | solution.py:107
  91.2 0.7 reshape.85
  91.9 12.2 %all-to-all-done = s32[64,1,2]{2,1,0:T(1,128)S(1)} async-done(((s32[64,1,2]{2,1,0:T(1,128)}), s32[64,1,2]{2,1,0:T(1,128)S(1)}, u32[]{:S(2)}, u32[]{:S(2)}) %all-to-all-start) | async-done | bytes 544 | tf_op jit(solution)/shard_map/all_to_all | solution.py:107
  104.2 5.7 %all-to-all-start.1 = ((f32[64,1,128]{2,1,0:T(1,128)}), f32[64,1,128]{2,1,0:T(1,128)S(1)}, u32[]{:S(2)}, u32[]{:S(2)}) async-start(f32[64,1,128]{2,1,0:T(1,128)} %reshape.85), calls=%async_computation.1 | async-start | bytes 65536 | tf_op jit(solution)/shard_map/all_to_all | solution.py:106
  110.4 0.7 reduce.3
  111.3 12.0 %all-to-all-done.1 = f32[64,1,128]{2,1,0:T(1,128)S(1)} async-done(((f32[64,1,128]{2,1,0:T(1,128)}), f32[64,1,128]{2,1,0:T(1,128)S(1)}, u32[]{:S(2)}, u32[]{:S(2)}) %all-to-all-start.1) | async-done | bytes 32800 | tf_op jit(solution)/shard_map/all_to_all | solution.py:106
  123.8 0.7 reduce.4
  124.7 0.8 fusion.21
  125.5 128.6 %all-gather.2.cloned.1.call-done = f32[4096,64]{1,0:T(8,128)} async-done(((f32[64,64]{1,0:T(8,128)}), f32[4096,64]{1,0:T(8,128)}) %all-gather.2.cloned.1.call-update) | async-done | bytes 1048592 | tf_op jit(solution)/shard_map/all_gather | solution.py:116
  254.1 2.2 gather_fusion
  256.8 4.8 %collective-permute-start.12 = (f32[1,8,64]{2,1,0:T(8,128)S(1)}, f32[1,8,64]{2,1,0:T(8,128)S(1)}, u32[]{:S(2)}, u32[]{:S(2)}) collective-permute-start(f32[1,8,64]{2,1,0:T(8,128)S(1)} %slice.187), channel_id=1, source_target_pairs={{8,0},{16,8},{24,16},{32,24},{40,32},{48,40},{56,48},{64,56},{72,6... | collective-permute-start | bytes 6152 | tf_op jit(solution)/shard_map/ppermute | solution.py:19
  261.6 1.4 fusion.1
  263.3 1.9 collective-permute-start.11
  265.2 1.6 fusion.20
  266.8 4.1 %collective-permute-done.11 = f32[1,8,64]{2,1,0:T(8,128)S(1)} collective-permute-done((f32[1,8,64]{2,1,0:T(8,128)S(1)}, f32[1,8,64]{2,1,0:T(8,128)S(1)}, u32[]{:S(2)}, u32[]{:S(2)}) %collective-permute-start.11) | collective-permute-done | bytes 2080 | tf_op jit(solution)/shard_map/ppermute | solution.py:16
  271.0 1.0 pad_maximum_fusion
  (79 shorter events, 4.8 us)
Async XLA Ops:
  7.2 1.0 copy-start
  7.2 14.0 %copy-start.11 = (s32[48,64]{1,0:T(8,128)S(1)}, s32[48,64]{1,0:T(8,128)}, u32[]{:S(2)}) copy-start(s32[48,64]{1,0:T(8,128)} %param.18) | copy-start | bytes 36868
  7.2 17.4 %copy-start.7 = (s32[48,1]{0,1:T(1,128)S(1)}, s32[48,1]{0,1:T(1,128)}, u32[]{:S(2)}) copy-start(s32[48,1]{0,1:T(1,128)} %param.21) | copy-start | bytes 580
  9.8 15.4 %collective-permute-start.1 = (f32[1,8,64]{2,1,0:T(8,128)S(1)}, f32[1,8,64]{2,1,0:T(8,128)S(1)}, u32[]{:S(2)}, u32[]{:S(2)}) collective-permute-start(f32[1,8,64]{2,1,0:T(8,128)S(1)} %slice.159), channel_id=1, source_target_pairs={{8,0},{16,8},{24,16},{32,24},{40,32},{48,40},{56,48},{64,56},{72,6... | collective-permute-start | bytes 6152 | tf_op jit(solution)/shard_map/ppermute | solution.py:19
  22.7 7.6 %collective-permute-start = (f32[1,8,64]{2,1,0:T(8,128)S(1)}, f32[1,8,64]{2,1,0:T(8,128)S(1)}, u32[]{:S(2)}, u32[]{:S(2)}) collective-permute-start(f32[1,8,64]{2,1,0:T(8,128)S(1)} %slice.155), channel_id=1, source_target_pairs={{0,8},{8,16},{16,24},{24,32},{32,40},{40,48},{48,56},{56,64},{64,7... | collective-permute-start | bytes 6152 | tf_op jit(solution)/shard_map/ppermute | solution.py:16
  24.9 5.4 %copy-start.1 = (bf16[48,8,512]{2,1,0:T(8,128)(2,1)S(1)}, bf16[48,8,512]{2,1,0:T(8,128)(2,1)}, u32[]{:S(2)}) copy-start(bf16[48,8,512]{2,1,0:T(8,128)(2,1)} %param.13) | copy-start | bytes 1179652
  24.9 5.4 %copy-start.3 = (f32[48,512]{1,0:T(8,128)S(1)}, f32[48,512]{1,0:T(8,128)}, u32[]{:S(2)}) copy-start(f32[48,512]{1,0:T(8,128)} %param.16) | copy-start | bytes 294916
  24.9 5.4 %copy-start.8 = (f32[48]{0:T(128)S(1)}, f32[48]{0:T(128)}, u32[]{:S(2)}) copy-start(f32[48]{0:T(128)} %param.15) | copy-start | bytes 580
  25.0 5.4 %copy-start.10 = (f32[8]{0:T(128)S(1)}, f32[8]{0:T(128)}, u32[]{:S(2)}) copy-start(f32[8]{0:T(128)} %param.14) | copy-start | bytes 100
  31.2 7.6 %collective-permute-start.3 = (f32[1,8,64]{2,1,0:T(8,128)S(1)}, f32[1,8,64]{2,1,0:T(8,128)S(1)}, u32[]{:S(2)}, u32[]{:S(2)}) collective-permute-start(f32[1,8,64]{2,1,0:T(8,128)S(1)} %slice.166), channel_id=1, source_target_pairs={{8,0},{16,8},{24,16},{32,24},{40,32},{48,40},{56,48},{64,56},{72,6... | collective-permute-start | bytes 6152 | tf_op jit(solution)/shard_map/ppermute | solution.py:19
  35.4 7.6 %collective-permute-start.2 = (f32[1,8,64]{2,1,0:T(8,128)S(1)}, f32[1,8,64]{2,1,0:T(8,128)S(1)}, u32[]{:S(2)}, u32[]{:S(2)}) collective-permute-start(f32[1,8,64]{2,1,0:T(8,128)S(1)} %slice.162), channel_id=1, source_target_pairs={{0,8},{8,16},{16,24},{24,32},{32,40},{40,48},{48,56},{56,64},{64,7... | collective-permute-start | bytes 6152 | tf_op jit(solution)/shard_map/ppermute | solution.py:16
  44.1 7.6 %collective-permute-start.5 = (f32[1,8,64]{2,1,0:T(8,128)S(1)}, f32[1,8,64]{2,1,0:T(8,128)S(1)}, u32[]{:S(2)}, u32[]{:S(2)}) collective-permute-start(f32[1,8,64]{2,1,0:T(8,128)S(1)} %slice.173), channel_id=1, source_target_pairs={{8,0},{16,8},{24,16},{32,24},{40,32},{48,40},{56,48},{64,56},{72,6... | collective-permute-start | bytes 6152 | tf_op jit(solution)/shard_map/ppermute | solution.py:19
  47.7 7.6 %collective-permute-start.4 = (f32[1,8,64]{2,1,0:T(8,128)S(1)}, f32[1,8,64]{2,1,0:T(8,128)S(1)}, u32[]{:S(2)}, u32[]{:S(2)}) collective-permute-start(f32[1,8,64]{2,1,0:T(8,128)S(1)} %slice.169), channel_id=1, source_target_pairs={{0,8},{8,16},{16,24},{24,32},{32,40},{40,48},{48,56},{56,64},{64,7... | collective-permute-start | bytes 6152 | tf_op jit(solution)/shard_map/ppermute | solution.py:16
  56.2 7.6 %collective-permute-start.7 = (f32[1,8,64]{2,1,0:T(8,128)S(1)}, f32[1,8,64]{2,1,0:T(8,128)S(1)}, u32[]{:S(2)}, u32[]{:S(2)}) collective-permute-start(f32[1,8,64]{2,1,0:T(8,128)S(1)} %slice.180), channel_id=1, source_target_pairs={{8,0},{16,8},{24,16},{32,24},{40,32},{48,40},{56,48},{64,56},{72,6... | collective-permute-start | bytes 6152 | tf_op jit(solution)/shard_map/ppermute | solution.py:19
  59.6 8.0 %copy-start.2 = (bf16[48,8,512]{2,1,0:T(8,128)(2,1)S(1)}, bf16[48,8,512]{2,1,0:T(8,128)(2,1)}, u32[]{:S(2)}) copy-start(bf16[48,8,512]{2,1,0:T(8,128)(2,1)} %param.12) | copy-start | bytes 1179652
  59.9 7.6 %collective-permute-start.6 = (f32[1,8,64]{2,1,0:T(8,128)S(1)}, f32[1,8,64]{2,1,0:T(8,128)S(1)}, u32[]{:S(2)}, u32[]{:S(2)}) collective-permute-start(f32[1,8,64]{2,1,0:T(8,128)S(1)} %slice.176), channel_id=1, source_target_pairs={{0,8},{8,16},{16,24},{24,32},{32,40},{40,48},{48,56},{56,64},{64,7... | collective-permute-start | bytes 6152 | tf_op jit(solution)/shard_map/ppermute | solution.py:16
  67.5 3.5 %copy-start.9 = (s32[48]{0:T(128)S(1)}, s32[48]{0:T(128)}, u32[]{:S(2)}) copy-start(s32[48]{0:T(128)} %param.22) | copy-start | bytes 580
  67.5 23.2 %copy-start.4 = (bf16[512,64]{0,1:T(8,128)(2,1)S(1)}, bf16[512,64]{0,1:T(8,128)(2,1)}, u32[]{:S(2)}) copy-start(bf16[512,64]{0,1:T(8,128)(2,1)} %param.19) | copy-start | bytes 196612
  67.5 57.1 %copy-start.6 = (f32[64,64]{1,0:T(8,128)S(1)}, f32[64,64]{1,0:T(8,128)}, u32[]{:S(2)}) copy-start(f32[64,64]{1,0:T(8,128)} %param.23) | copy-start | bytes 49156
  69.0 187.2 %copy-start.5 = (bf16[64,512]{1,0:T(8,128)(2,1)S(1)}, bf16[64,512]{1,0:T(8,128)(2,1)}, u32[]{:S(2)}) copy-start(bf16[64,512]{1,0:T(8,128)(2,1)} %param.20) | copy-start | bytes 196612
  69.0 3.3 %collective-permute-start.8 = (f32[48,512]{1,0:T(8,128)S(1)}, f32[48,512]{1,0:T(8,128)S(1)}, u32[]{:S(2)}, u32[]{:S(2)}) collective-permute-start(f32[48,512]{1,0:T(8,128)S(1)} %get-tuple-element.3), channel_id=1, source_target_pairs={{0,1},{1,0},{2,3},{3,2},{4,5},{5,4},{6,7},{7,6},{8,9},{9,8},{10,11... | collective-permute-start | bytes 294920 | tf_op jit(solution)/shard_map/ppermute | solution.py:83
  72.3 6.7 %collective-permute-start.9 = (f32[48,512]{1,0:T(8,128)S(1)}, f32[48,512]{1,0:T(8,128)S(1)}, u32[]{:S(2)}, u32[]{:S(2)}) collective-permute-start(f32[48,512]{1,0:T(8,128)S(1)} %add.120), channel_id=1, source_target_pairs={{0,2},{1,3},{2,0},{3,1},{4,6},{5,7},{6,4},{7,5},{8,10},{9,11},{10,... | collective-permute-start | bytes 294920 | tf_op jit(solution)/shard_map/ppermute | solution.py:83
  79.1 11.6 %collective-permute-start.10 = (f32[48,512]{1,0:T(8,128)S(1)}, f32[48,512]{1,0:T(8,128)S(1)}, u32[]{:S(2)}, u32[]{:S(2)}) collective-permute-start(f32[48,512]{1,0:T(8,128)S(1)} %add.121), channel_id=1, source_target_pairs={{0,4},{1,5},{2,6},{3,7},{4,0},{5,1},{6,2},{7,3},{8,12},{9,13},{10,... | collective-permute-start | bytes 294920 | tf_op jit(solution)/shard_map/ppermute | solution.py:83
  85.0 19.2 %all-to-all-start = ((s32[64,1,2]{2,1,0:T(1,128)}), s32[64,1,2]{2,1,0:T(1,128)S(1)}, u32[]{:S(2)}, u32[]{:S(2)}) async-start(s32[64,1,2]{2,1,0:T(1,128)} %bitcast.2), calls=%async_computation | async-start | bytes 65536 | tf_op jit(solution)/shard_map/all_to_all | solution.py:107
  104.2 19.1 %all-to-all-start.1 = ((f32[64,1,128]{2,1,0:T(1,128)}), f32[64,1,128]{2,1,0:T(1,128)S(1)}, u32[]{:S(2)}, u32[]{:S(2)}) async-start(f32[64,1,128]{2,1,0:T(1,128)} %reshape.85), calls=%async_computation.1 | async-start | bytes 65536 | tf_op jit(solution)/shard_map/all_to_all | solution.py:106
  109.8 144.2 %all-gather.2.cloned.1.call-start = ((), (), s32[]{:S(2)}) async-start(), calls=%async_computation.2 | async-start | bytes 2129920 | tf_op jit(solution)/shard_map/all_gather | solution.py:116
  256.8 8.4 %collective-permute-start.12 = (f32[1,8,64]{2,1,0:T(8,128)S(1)}, f32[1,8,64]{2,1,0:T(8,128)S(1)}, u32[]{:S(2)}, u32[]{:S(2)}) collective-permute-start(f32[1,8,64]{2,1,0:T(8,128)S(1)} %slice.187), channel_id=1, source_target_pairs={{8,0},{16,8},{24,16},{32,24},{40,32},{48,40},{56,48},{64,56},{72,6... | collective-permute-start | bytes 6152 | tf_op jit(solution)/shard_map/ppermute | solution.py:19
  263.3 7.6 %collective-permute-start.11 = (f32[1,8,64]{2,1,0:T(8,128)S(1)}, f32[1,8,64]{2,1,0:T(8,128)S(1)}, u32[]{:S(2)}, u32[]{:S(2)}) collective-permute-start(f32[1,8,64]{2,1,0:T(8,128)S(1)} %slice.183), channel_id=1, source_target_pairs={{0,8},{8,16},{16,24},{24,32},{32,40},{40,48},{48,56},{56,64},{64,7... | collective-permute-start | bytes 6152 | tf_op jit(solution)/shard_map/ppermute | solution.py:16
Sparse Core Ops, SparseCore 0:
  125.6 128.4 all-gather.1
